TPU v7x, 32 devices: a whole 2x2x4 slice. The times are simulated.
32 devices in a mesh: section: 2 (over core), dp: 16 (over z, y, x).
Axes of the slice: x: 2, y: 2, z: 4, core: 2. Of those that a mesh axis runs over, the one named last changes fastest.
Arguments:
- tokens: bfloat16 [8192, 1024], P('dp'), may hold values from -6 to 6
- cotangent: bfloat16 [8192, 1024], P('dp'), may hold values from -6 to 6
- lengths: int32 [16, 2, 4], P('dp'), may hold values from 1 to 128, 256 in all within a row
- w_in: bfloat16 [2, 1024, 3352], P('section'), may hold values from -0.1875 to 0.1875
- conv_w: float32 [2, 4, 1792], P('section'), may hold values from -4 to 4
- conv_b: float32 [2, 1792], P('section'), may hold values from -3 to 3
- dt_bias: float32 [2, 24], P('section'), may hold values from -3 to 0.5
- a_log: float32 [2, 24], P('section'), may hold values from -3 to 1
- d_skip: float32 [2, 24], P('section'), may hold values from 0.3 to 1.5
- g_mix: float32 [2, 1024], P('section'), may hold values from 0.25 to 1.75
- g_ssm: float32 [2, 1536], P('section'), may hold values from 0.25 to 1.75
- w_out: bfloat16 [2, 1536, 1024], P('section'), may hold values from -0.15625 to 0.15625
- w_qkv: bfloat16 [2, 1024, 768], P('section'), may hold values from -0.1875 to 0.1875
- w_o: bfloat16 [2, 512, 1024], P('section'), may hold values from -0.75 to 0.75
- g_ffn: float32 [2, 1024], P('section'), may hold values from 0.25 to 1.75
- w_gu: bfloat16 [2, 1024, 4096], P('section'), may hold values from -0.1875 to 0.1875
- w_down: bfloat16 [2, 2048, 1024], P('section'), may hold values from -0.125 to 0.125
Outputs:
- layer_out: bfloat16 [2, 8192, 1024], P('section', 'dp')
- input_grad: bfloat16 [2, 8192, 1024], P('section', 'dp')
- grad_w_in: float32 [2, 1024, 3352], P('section', 'dp')
- grad_conv_w: float32 [2, 4, 1792], P('section')
- grad_conv_b: float32 [2, 1792], P('section')
- grad_dt_bias: float32 [2, 24], P('section')
- grad_a_log: float32 [2, 24], P('section')
- grad_d_skip: float32 [2, 24], P('section')
- grad_g_mix: float32 [2, 1024], P('section', 'dp')
- grad_g_ssm: float32 [2, 1536], P('section', 'dp')
- grad_w_out: float32 [2, 1536, 1024], P('section', 'dp')
- grad_w_qkv: float32 [2, 1024, 768], P('section', 'dp')
- grad_w_o: float32 [2, 512, 1024], P('section', 'dp')
- grad_g_ffn: float32 [2, 1024], P('section', 'dp')
- grad_w_gu: float32 [2, 1024, 4096], P('section', 'dp')
- grad_w_down: float32 [2, 2048, 1024], P('section', 'dp')
Inputs may be any that keep to these rules, and one draw needn't show every extreme that they name: `lengths`: each row sums to 256; the longest sequence of each micro-batch has 128 tokens.
All inputs are finite; a program needn't handle non-finite values.
Results may differ from a plain program's by a relative error of at most 0.028.
Values may be sent and summed in bfloat16 or wider, within the bound.
A program may use at most 320 MiB of HBM per device.

v0:
```python
import jax
import jax.numpy as jnp
from jax import lax
from jax.sharding import PartitionSpec as P

D = 1024
NH = 24
MH = 64
NS = 128
QH = 8
KVH = 2
AH = 64
FF = 2048
CONV = 4
MICRO = 2
MB_TOK = 256
DI = 1536


epsilon = 1e-05
ROPE_BASE = 10000.0


def passed_along(block, axis, distance):
    devices = range(lax.axis_size(axis))
    route = [(i - distance, i) for i in devices if i - distance in devices]
    return lax.ppermute(block, axis, route)


def round_value(values):
    rounded = values.astype(jnp.bfloat16).astype(jnp.float32)
    return values + lax.stop_gradient(rounded - values)


def round_plain(values):
    return values.astype(jnp.bfloat16).astype(jnp.float32)


def product(left, right):
    return jnp.dot(left, right, precision=lax.Precision.HIGHEST)


def rms_norm(values, gain):
    return values * lax.rsqrt(jnp.mean(values * values, axis=-1, keepdims=True) + epsilon) * gain


def rotate(values, position):
    half = values.shape[-1] // 2
    freq = ROPE_BASE ** (-jnp.arange(half).astype(jnp.float32) / half)
    angle = position[:, None] * freq[None, :]
    cosine = jnp.cos(angle)[:, None, :]
    sine = jnp.sin(angle)[:, None, :]
    first = values[..., :half]
    second = values[..., half:]
    return jnp.concatenate([first * cosine - second * sine, second * cosine + first * sine], -1)


def segments(row):
    ends = jnp.cumsum(row)
    place = jnp.arange(MB_TOK)
    return jnp.sum((place[:, None] >= ends[None, :]).astype(jnp.int32), axis=1)


def layer(x, doc_ids, params):
    (
        w_in,
        conv_w,
        conv_b,
        dt_bias,
        a_log,
        d_skip,
        g_mix,
        g_ssm,
        w_out,
        w_qkv,
        w_o,
        g_ffn,
        w_gu,
        w_down,
    ) = params
    count = x.shape[0]
    place = jnp.arange(count)
    visible = (doc_ids[:, None] == doc_ids[None, :]) & (place[:, None] >= place[None, :])
    position = jnp.sum(visible.astype(jnp.int32), axis=1) - 1
    normed = round_value(rms_norm(x, g_mix))
    projected = product(normed, w_in)
    gate_z = projected[:, :DI]
    conv_in = projected[:, DI : 2 * DI + 2 * NS]
    step_raw = projected[:, 2 * DI + 2 * NS :]
    conv = conv_b[None, :] + conv_w[0][None, :] * conv_in
    for lag in range(1, CONV):
        moved = jnp.concatenate(
            [jnp.zeros((lag, conv_in.shape[1]), conv_in.dtype), conv_in[: count - lag]], 0
        )
        keep_rows = (position >= lag).astype(conv_in.dtype)
        conv = conv + conv_w[lag][None, :] * moved * keep_rows[:, None]
    conv = jax.nn.silu(conv)
    ssm_in = conv[:, :DI].reshape(count, NH, MH)
    b_proj = conv[:, DI : DI + NS]
    c_proj = conv[:, DI + NS :]
    step_size = jax.nn.softplus(step_raw + dt_bias[None, :])
    decay_sum = jnp.cumsum(step_size * (-jnp.exp(a_log))[None, :], axis=0)
    cb_scores = product(c_proj, b_proj.T)
    inside = visible[:, :, None]
    log_gap = jnp.where(inside, decay_sum[:, None, :] - decay_sum[None, :, :], 0.0)
    mix_weight = (
        jnp.where(inside, jnp.exp(log_gap), 0.0) * cb_scores[:, :, None] * step_size[None, :, :]
    )
    ssm_out = jnp.einsum("tsh,shp->thp", mix_weight, ssm_in, precision=lax.Precision.HIGHEST)
    ssm_out = ssm_out + d_skip[None, :, None] * ssm_in
    ssm_out = ssm_out.reshape(count, DI) * jax.nn.silu(gate_z)
    mixer = product(round_value(rms_norm(ssm_out, g_ssm)), w_out)
    qkv = product(normed, w_qkv)
    angle_pos = position.astype(jnp.float32)
    query = rotate(qkv[:, : QH * AH].reshape(count, QH, AH), angle_pos).reshape(
        count, KVH, QH // KVH, AH
    )
    key = rotate(qkv[:, QH * AH : (QH + KVH) * AH].reshape(count, KVH, AH), angle_pos)
    value = qkv[:, (QH + KVH) * AH :].reshape(count, KVH, AH)
    query = round_value(query)
    key = round_value(key)
    value = round_value(value)
    scores = jnp.einsum("tgqa,sga->gqts", query, key, precision=lax.Precision.HIGHEST) * AH ** (
        -0.5
    )
    scores = jnp.where(visible[None, None], scores, -1e30)
    probs = round_value(jax.nn.softmax(scores, axis=-1))
    context = jnp.einsum("gqts,sga->tgqa", probs, value, precision=lax.Precision.HIGHEST).reshape(
        count, QH * AH
    )
    attended = product(round_value(context), w_o)
    middle = x + mixer + attended
    ffn_in = round_value(rms_norm(middle, g_ffn))
    both = product(ffn_in, w_gu)
    action = round_value(jax.nn.silu(both[:, :FF]) * both[:, FF:])
    return round_value(middle + product(action, w_down))


def partial_layer(docs_here):

    def apply_layer(layer_in, params):
        return layer(layer_in, docs_here, params)

    return apply_layer


def local(
    tokens,
    cotangent,
    lengths,
    w_in,
    conv_w,
    conv_b,
    dt_bias,
    a_log,
    d_skip,
    g_mix,
    g_ssm,
    w_out,
    w_qkv,
    w_o,
    g_ffn,
    w_gu,
    w_down,
):
    first = lax.axis_index("section") == 0
    weights = (
        w_in,
        conv_w,
        conv_b,
        dt_bias,
        a_log,
        d_skip,
        g_mix,
        g_ssm,
        w_out,
        w_qkv,
        w_o,
        g_ffn,
        w_gu,
        w_down,
    )
    params = tuple((w[0].astype(jnp.float32) for w in weights))
    inputs = tokens.astype(jnp.float32).reshape(MICRO, MB_TOK, D)
    incoming = cotangent.astype(jnp.float32).reshape(MICRO, MB_TOK, D)
    doc_table = jnp.stack([segments(lengths[0, index]) for index in range(MICRO)])
    large_index = (0, 6, 7, 8, 9, 10, 11, 12, 13)
    small_index = (1, 2, 3, 4, 5)
    received = jnp.zeros((MB_TOK, D), jnp.float32)
    results = []
    backers = []
    for tick in range(MICRO + 1):
        fresh = inputs[min(tick, MICRO - 1)]
        layer_in = jnp.where(first, fresh, received)
        docs_here = jnp.where(first, doc_table[min(tick, MICRO - 1)], doc_table[max(tick - 1, 0)])
        result, backer = jax.vjp(partial_layer(docs_here), layer_in, params)
        results.append(result)
        backers.append(backer)
        if tick < MICRO:
            received = passed_along(result.astype(jnp.bfloat16), "section", 1).astype(jnp.float32)
    returned = jnp.zeros((MB_TOK, D), jnp.float32)
    input_grads = [None] * (MICRO + 1)
    local_large = [jnp.zeros_like(params[i]) for i in large_index]
    local_small = [jnp.zeros_like(params[i]) for i in small_index]
    summed_large = None
    for tick in reversed(range(MICRO + 1)):
        if tick >= 1:
            seed_grad = incoming[tick - 1]
        else:
            seed_grad = jnp.zeros((MB_TOK, D), jnp.float32)
        upstream = jnp.where(first, returned, seed_grad)
        grad_raw, grads = backers[tick](upstream)
        grad_in = round_plain(grad_raw)
        input_grads[tick] = grad_in
        if tick > 0:
            returned = passed_along(grad_in.astype(jnp.bfloat16), "section", -1).astype(jnp.float32)
        local_small = [total + grads[i] for total, i in zip(local_small, small_index)]
        local_large = [total + grads[i] for total, i in zip(local_large, large_index)]
    summed_large = list(
        lax.psum_scatter(
            tuple((g[None] for g in local_large)), "dp", scatter_dimension=1, tiled=True
        )
    )
    summed_small = lax.psum(tuple((g[None] for g in local_small)), "dp")
    out_rows = [jnp.where(first, results[index], results[index + 1]) for index in range(MICRO)]
    grad_rows = [
        jnp.where(first, input_grads[index], input_grads[index + 1]) for index in range(MICRO)
    ]
    layer_out = jnp.concatenate(out_rows, 0)[None].astype(jnp.bfloat16)
    input_grad = jnp.concatenate(grad_rows, 0)[None].astype(jnp.bfloat16)
    (
        grad_w_in,
        grad_g_mix,
        grad_g_ssm,
        grad_w_out,
        grad_w_qkv,
        grad_w_o,
        grad_g_ffn,
        grad_w_gu,
        grad_w_down,
    ) = summed_large
    grad_conv_w, grad_conv_b, grad_dt_bias, grad_a_log, grad_d_skip = summed_small
    return (
        layer_out,
        input_grad,
        grad_w_in,
        grad_conv_w,
        grad_conv_b,
        grad_dt_bias,
        grad_a_log,
        grad_d_skip,
        grad_g_mix,
        grad_g_ssm,
        grad_w_out,
        grad_w_qkv,
        grad_w_o,
        grad_g_ffn,
        grad_w_gu,
        grad_w_down,
    )


def solution(mesh):
    in_specs = (
        P("dp", None),
        P("dp", None),
        P("dp", None, None),
        P("section", None, None),
        P("section", None, None),
        P("section", None),
        P("section", None),
        P("section", None),
        P("section", None),
        P("section", None),
        P("section", None),
        P("section", None, None),
        P("section", None, None),
        P("section", None, None),
        P("section", None),
        P("section", None, None),
        P("section", None, None),
    )
    out_specs = (
        P("section", "dp", None),
        P("section", "dp", None),
        P("section", "dp", None),
        P("section", None, None),
        P("section", None),
        P("section", None),
        P("section", None),
        P("section", None),
        P("section", "dp"),
        P("section", "dp"),
        P("section", "dp", None),
        P("section", "dp", None),
        P("section", "dp", None),
        P("section", "dp"),
        P("section", "dp", None),
        P("section", "dp", None),
    )
    return jax.shard_map(local, mesh=mesh, in_specs=in_specs, out_specs=out_specs, check_vma=False)
```

profile of v0, /device:TPU:10, one launch (start us, length us, event | category | flops | bytes accessed | tf_op | source)
XLA Modules:
  0.0 2091.1 jit_solution(17464091502492595509)
XLA Ops:
  18.5 8.8 fusion.22
  31.7 6.3 fusion.150
  57.4 10.1 bitcast_add_fusion.5
  85.4 7.1 fusion.10
  104.7 8.7 fusion.20
  126.4 9.7 bitcast_add_fusion.4
  161.0 10.6 fusion.8
  187.5 8.9 fusion.18
  209.3 9.9 bitcast_add_fusion.3
  243.4 11.2 fusion.6
  254.6 6.0 fusion.472
  260.7 7.5 multiply_reduce_fusion.32
  288.2 10.8 fusion.63
  305.6 8.0 bitcast_add_fusion.2
  325.4 6.2 fusion.16
  337.1 15.5 fusion.116
  352.7 6.3 fusion.469
  359.1 7.5 multiply_reduce_fusion.31
  388.7 10.8 fusion.65
  404.7 7.7 bitcast_add_fusion.1
  424.4 6.2 fusion.14
  437.0 15.7 fusion.117
  457.0 7.1 multiply_reduce_fusion.30
  487.9 11.0 fusion.67
  508.1 7.7 bitcast_add_fusion
  527.7 6.2 fusion.12
  541.5 21.5 %add_bitcast_fusion.1 = f32[1,1024,3352]{1,2,0:T(8,128)} fusion(f32[1024,3352]{0,1:T(8,128)} %fusion.116, f32[1024,3352]{0,1:T(8,128)} %fusion.117, f32[256,1536]{0,1:T(8,128)} %get-tuple-element.194, f32[256,1792]{0,1:T(8,128)} %copy-done.75, f32[256,24]{0,1:T(8,128)S(1)} %copy-done.215, f32[1024]{0:T(1024)S(1)} %bitcast.746, f32[256]{0:T(256)S(1)} %copy-done.241, ...), kind=kOutput, calls=%fused_computation.1 | convolution fusion | flops 10554896384 | bytes 45675520 | tf_op jit(solution)/shard_map/transpose(jvp())/dot_general | solution.py:40
  563.0 32.2 %copy.208 = f32[1,1024,3352]{2,0,1:T(1,128)} copy(f32[1,1024,3352]{1,2,0:T(8,128)} %add_bitcast_fusion.1) | data formatting | bytes 27459584 | tf_op jit(solution)/shard_map/broadcast_in_dim | solution.py:221
  606.8 6.8 fusion.276
  613.7 5.3 fusion.277
  619.0 7.4 add_bitcast_fusion.4
  627.0 7.4 fusion.238
  634.6 5.6 fusion.237
  640.2 8.2 add_bitcast_fusion.3
  648.5 10.0 fusion.210
  658.5 7.8 fusion.203
  666.4 12.6 add_bitcast_fusion.2
  679.6 19.2 fusion.60
  698.9 16.8 fusion.61
  715.7 24.7 %add_bitcast_fusion = f32[1,1024,4096]{2,1,0:T(8,128)} fusion(f32[1024,4096]{1,0:T(8,128)} %fusion.60, f32[1024,4096]{1,0:T(8,128)} %fusion.61, f32[256,2048]{1,0:T(8,128)} %copy-done.109, f32[256,2048]{1,0:T(8,128)} %copy-done.108, f32[256,1024]{1,0:T(8,128)} %copy-done.70, f32[1024]{0:T(1024)S(1)} %bitcast.797, f32[256]{0:T(256)S(1)} %copy-done.306), kind=kOutput, calls=%fused_computation | convolution fusion | flops 12895911936 | bytes 55579648 | tf_op jit(solution)/shard_map/transpose(jvp())/dot_general | solution.py:40
  745.3 7.9 fusion.281
  755.3 66.2 %all-reduce.76 = (f32[1,4,1792]{2,1,0:T(4,128)}, f32[1,1792]{1,0:T(1,128)}, f32[1,24]{1,0:T(1,128)}, f32[1,24]{1,0:T(1,128)}, f32[1,24]{1,0:T(1,128)}) all-reduce(f32[1,4,1792]{2,1,0:T(4,128)S(1)} %add_bitcast_fusion.6, f32[1,1792]{1,0:T(1,128)S(1)} %add.863, ...), channel_id=1, replica_groups=mesh['section'=2,'dp'=16] {'dp'}, use_global_device_ids=true, to_apply=%region_71.73 | all-reduce | flops 9032 | bytes 72256 | tf_op jit(solution)/shard_map/psum | solution.py:224
  829.5 349.1 %all-reduce.79.cloned.1.call-done = f32[1,1024,3352]{2,0,1:T(1,128)} async-done(((f32[1,1024,3352]{2,0,1:T(1,128)}), f32[1,1024,3352]{2,0,1:T(1,128)}) %all-reduce.79.cloned.1.call-update) | async-done | bytes 13729808
  1180.8 71.9 %reduce-scatter.19.cloned.1.call-done = f32[1,32,1024]{2,1,0:T(8,128)} async-done(((f32[1,512,1024]{2,1,0:T(8,128)}), f32[1,32,1024]{2,1,0:T(8,128)}) %reduce-scatter.19.cloned.1.call-update) | async-done | bytes 131088 | tf_op jit(solution)/shard_map/reduce_scatter | solution.py:220
  1252.7 143.0 %reduce-scatter.17.cloned.1.call-done = f32[1,64,768]{2,1,0:T(8,128)} async-done(((f32[1,1024,768]{2,1,0:T(8,128)}), f32[1,64,768]{2,1,0:T(8,128)}) %reduce-scatter.17.cloned.1.call-update) | async-done | bytes 196624 | tf_op jit(solution)/shard_map/reduce_scatter | solution.py:220
  1395.7 151.1 %reduce-scatter.15.cloned.1.call-done = f32[1,96,1024]{2,1,0:T(8,128)} async-done(((f32[1,1536,1024]{2,1,0:T(8,128)}), f32[1,96,1024]{2,1,0:T(8,128)}) %reduce-scatter.15.cloned.1.call-update) | async-done | bytes 393232 | tf_op jit(solution)/shard_map/reduce_scatter | solution.py:220
  1546.8 183.3 %reduce-scatter.23.cloned.1.call-done = f32[1,128,1024]{2,1,0:T(8,128)} async-done(((f32[1,2048,1024]{2,1,0:T(8,128)}), f32[1,128,1024]{2,1,0:T(8,128)}) %reduce-scatter.23.cloned.1.call-update) | async-done | bytes 524304 | tf_op jit(solution)/shard_map/reduce_scatter | solution.py:220
  1730.1 354.2 %reduce-scatter.21.cloned.1.call-done = f32[1,64,4096]{2,1,0:T(8,128)} async-done(((f32[1,1024,4096]{2,1,0:T(8,128)}), f32[1,64,4096]{2,1,0:T(8,128)}) %reduce-scatter.21.cloned.1.call-update) | async-done | bytes 1048592 | tf_op jit(solution)/shard_map/reduce_scatter | solution.py:220
  (1074 shorter events, 327.6 us)
Async XLA Ops:
  7.2 73.4 %copy-start = (bf16[1,1536,1024]{2,1,0:T(8,128)(2,1)S(1)}, bf16[1,1536,1024]{2,1,0:T(8,128)(2,1)}, u32[]{:S(2)}) copy-start(bf16[1,1536,1024]{2,1,0:T(8,128)(2,1)} %param.29) | copy-start | bytes 9437188
  7.2 818.2 %reduce-scatter.29.cloned.1.call-start = ((), (), s32[]{:S(2)}) async-start(), calls=%async_computation.15 | async-start | bytes 557056
  11.3 31.6 %copy-start.337 = (s32[256]{0:T(256)}, s32[256]{0:T(256)S(1)}, u32[]{:S(2)}) copy-start(s32[256]{0:T(256)S(1)} %convert_reduce_fusion) | copy-start | bytes 3076
  11.3 31.4 %copy-start.270 = (s32[256]{0:T(256)}, s32[256]{0:T(256)S(1)}, u32[]{:S(2)}) copy-start(s32[256]{0:T(256)S(1)} %broadcast_select_fusion) | copy-start | bytes 3076
  18.5 59.2 %copy-start.120 = (pred[256,256]{0,1:T(8,128)(4,1)}, pred[256,256]{0,1:T(8,128)(4,1)S(1)}, u32[]{:S(2)}) copy-start(pred[256,256]{0,1:T(8,128)(4,1)S(1)} %get-tuple-element.252) | copy-start | bytes 196612
  44.7 22.9 %copy-start.137 = (f32[256,32]{0,1:T(8,128)}, f32[256,32]{0,1:T(8,128)S(1)}, u32[]{:S(2)}) copy-start(f32[256,32]{0,1:T(8,128)S(1)} %get-tuple-element.270) | copy-start | bytes 98308
  44.7 22.9 %copy-start.139 = (f32[256,32]{0,1:T(8,128)}, f32[256,32]{0,1:T(8,128)S(1)}, u32[]{:S(2)}) copy-start(f32[256,32]{0,1:T(8,128)S(1)} %get-tuple-element.271) | copy-start | bytes 98308
  50.3 17.2 copy-start.288
  97.7 4.9 collective-permute-start
  104.1 17.9 copy-start.34
  104.7 17.4 copy-start.232
  153.2 31.9 %copy-start.227 = (f32[2,4,256]{2,1,0:T(4,128)}, f32[2,4,256]{2,1,0:T(4,128)S(1)}, u32[]{:S(2)}) copy-start(f32[2,4,256]{2,1,0:T(4,128)S(1)} %fusion.242) | copy-start | bytes 24580
  176.4 9.4 collective-permute-start.1
  178.7 18.3 copy-start.319
  178.7 18.3 copy-start.321
  178.7 18.3 copy-start.323
  187.4 17.7 copy-start.38
  187.4 17.7 copy-start.235
  243.3 24.9 %copy-start.97 = (f32[256,1024]{1,0:T(8,128)}, f32[256,1024]{1,0:T(8,128)S(1)}, u32[]{:S(2)}) copy-start(f32[256,1024]{1,0:T(8,128)S(1)} %get-tuple-element.291) | copy-start | bytes 3145732
  243.3 24.9 %copy-start.297 = (f32[256]{0:T(256)}, f32[256]{0:T(256)S(1)}, u32[]{:S(2)}) copy-start(f32[256]{0:T(256)S(1)} %fusion.415) | copy-start | bytes 3076
  243.3 17.3 slice-start.2
  305.6 19.7 slice-start.8
  335.5 17.2 copy-start.73
  335.5 17.2 copy-start.360
  335.5 17.1 collective-permute-start.2
  337.1 21.9 %slice-start.4 = ((s8[8388608]{0:T(1024)(128)(4,1)}), s8[4194304]{0:T(1024)(128)(4,1)S(1)}, s32[]{:S(2)}) async-start(s8[8388608]{0:T(1024)(128)(4,1)} %bitcast.842), calls=%async_computation.21 | async-start | bytes 8388608
  404.7 19.7 slice-start.10
  435.5 17.3 copy-start.116
  435.5 17.4 copy-start.131
  435.5 17.4 copy-start.361
  435.5 17.4 collective-permute-start.3
  437.0 19.9 slice-start.6
  501.4 325.3 %reduce-scatter.25.cloned.1.call-start = ((), (), s32[]{:S(2)}) async-start(), calls=%async_computation.13 | async-start | bytes 557056
  508.1 19.6 slice-start.12
  539.5 288.6 %reduce-scatter.27.cloned.1.call-start = ((), (), s32[]{:S(2)}) async-start(), calls=%async_computation.14 | async-start | bytes 835584
  541.4 637.2 %all-reduce.79.cloned.1.call-start = ((), (), s32[]{:S(2)}) async-start(), calls=%async_computation.16 | async-start | bytes 28311552
  595.2 657.5 %reduce-scatter.19.cloned.1.call-start = ((), (), s32[]{:S(2)}) async-start(), calls=%async_computation.10 | async-start | bytes 2228224 | tf_op jit(solution)/shard_map/reduce_scatter | solution.py:220
  605.9 789.8 %reduce-scatter.17.cloned.1.call-start = ((), (), s32[]{:S(2)}) async-start(), calls=%async_computation.9 | async-start | bytes 3342336 | tf_op jit(solution)/shard_map/reduce_scatter | solution.py:220
  626.4 920.4 %reduce-scatter.15.cloned.1.call-start = ((), (), s32[]{:S(2)}) async-start(), calls=%async_computation.8 | async-start | bytes 6684672 | tf_op jit(solution)/shard_map/reduce_scatter | solution.py:220
  648.4 1081.7 %reduce-scatter.23.cloned.1.call-start = ((), (), s32[]{:S(2)}) async-start(), calls=%async_computation.12 | async-start | bytes 8912896 | tf_op jit(solution)/shard_map/reduce_scatter | solution.py:220
  679.0 19.8 copy-start.303
  679.0 1405.4 %reduce-scatter.21.cloned.1.call-start = ((), (), s32[]{:S(2)}) async-start(), calls=%async_computation.11 | async-start | bytes 17825792 | tf_op jit(solution)/shard_map/reduce_scatter | solution.py:220
  679.6 19.2 copy-start.100
  679.6 19.2 copy-start.105
  679.6 19.2 copy-start.107
  753.4 68.1 %copy-start.326 = (f32[256]{0:T(256)S(1)}, f32[256]{0:T(256)}, u32[]{:S(2)}) copy-start(f32[256]{0:T(256)} %copy-done.325) | copy-start | bytes 3076
  753.4 68.1 %copy-start.348 = (f32[256]{0:T(256)S(1)}, f32[256]{0:T(256)}, u32[]{:S(2)}) copy-start(f32[256]{0:T(256)} %get-tuple-element.111) | copy-start | bytes 3076
  753.4 68.1 %copy-start.243 = (f32[256]{0:T(256)S(1)}, f32[256]{0:T(256)}, u32[]{:S(2)}) copy-start(f32[256]{0:T(256)} %copy-done.239) | copy-start | bytes 3076
  (346 other events, 1632.2 us)
Sparse Core Ops, SparseCore 0:
  501.5 67.8 reduce-scatter.28
  571.7 72.9 reduce-scatter.24
  650.0 129.2 reduce-scatter.26
  785.6 392.9 all-reduce.78
  1181.3 71.3 reduce-scatter.18
  1258.1 137.5 reduce-scatter.16
  1401.5 145.2 reduce-scatter.14
  1549.7 180.3 reduce-scatter.22
  1733.0 351.3 reduce-scatter.20
where the time goes:
time: 2100 us; the launch traced here: 2090 us
  waiting for transfers between devices  1250 us (60%)
  matrix products  507 us (24%)
  other arithmetic  139 us (7%)
  local copies, waits for them, and re-layouts  97.9 us (5%)
  blocking collectives  66.2 us (3%)
    reduce_scatter x5, waiting for transfers between devices, local(): lax.psum_scatter(tuple((g[None] for g in local_large)), 'dp', scatter_dim...  904 us
    dot_general x63, matrix products, product(): return jnp.dot(left, right, precision=lax.Precision.HIGHEST)  375 us
    unnamed x13, waiting for transfers between devices  349 us
    dot_general x9, matrix products, layer(): jnp.einsum('tsh,shp->thp', mix_weight, ssm_in, precision=lax.Precision.HI...  85.7 us
    psum x1, blocking collectives, local(): summed_small = lax.psum(tuple((g[None] for g in local_small)), 'dp')  66.2 us
  transfers between devices with their start and end apart: 13, of which 6 were waited for; matrix products, arithmetic and copies ran while one was open for 14% of the time, Pallas kernels for 0%

commit v1 on v0

v1 whole, which is shorter than its diff:
```python
import jax
import jax.numpy as jnp
from jax import lax
from jax.sharding import PartitionSpec as P

D = 1024
NH = 24
MH = 64
NS = 128
QH = 8
KVH = 2
AH = 64
FF = 2048
CONV = 4
MICRO = 2
MB_TOK = 256
DI = 1536


epsilon = 1e-05
ROPE_BASE = 10000.0


def passed_along(block, axis, distance):
    devices = range(lax.axis_size(axis))
    route = [(i - distance, i) for i in devices if i - distance in devices]
    return lax.ppermute(block, axis, route)


@jax.custom_vjp
def round_value(values):
    return values.astype(jnp.bfloat16).astype(jnp.float32)


round_value.defvjp(lambda values: (round_value(values), None), lambda kept, grad: (grad,))


def round_plain(values):
    return values.astype(jnp.bfloat16).astype(jnp.float32)


@jax.custom_vjp
def tapped(values, probe):
    return values


tapped.defvjp(lambda values, probe: (values, None), lambda kept, grad: (grad, grad))


@jax.custom_vjp
def product(left, weight):
    return jnp.dot(left.astype(jnp.bfloat16), weight, preferred_element_type=jnp.float32)


def product_back(weight, grad):
    back = lax.dot_general(
        grad.astype(jnp.bfloat16),
        weight,
        (((1,), (1,)), ((), ())),
        preferred_element_type=jnp.float32,
    )
    return back, jnp.zeros_like(weight)


product.defvjp(lambda left, weight: (product(left, weight), weight), product_back)


def contract(spec, left, right):
    return jnp.einsum(spec, left, right, precision=lax.Precision.DEFAULT)


def rms_norm(values, gain):
    return values * lax.rsqrt(jnp.mean(values * values, axis=-1, keepdims=True) + epsilon) * gain


def rotate(values, position):
    half = values.shape[-1] // 2
    freq = ROPE_BASE ** (-jnp.arange(half).astype(jnp.float32) / half)
    angle = position[:, None] * freq[None, :]
    cosine = jnp.cos(angle)[:, None, :]
    sine = jnp.sin(angle)[:, None, :]
    first = values[..., :half]
    second = values[..., half:]
    return jnp.concatenate([first * cosine - second * sine, second * cosine + first * sine], -1)


def segments(row):
    ends = jnp.cumsum(row)
    place = jnp.arange(MB_TOK)
    return jnp.sum((place[:, None] >= ends[None, :]).astype(jnp.int32), axis=1)


def layer(x, small, probes, doc_ids, large):
    conv_w, conv_b, dt_bias, a_log, d_skip, g_mix, g_ssm, g_ffn = small
    w_in, w_out, w_qkv, w_o, w_gu, w_down = large
    count = x.shape[0]
    place = jnp.arange(count)
    earlier = place[:, None] >= place[None, :]
    visible = (doc_ids[:, None] == doc_ids[None, :]) & earlier
    position = jnp.sum(visible.astype(jnp.int32), axis=1) - 1
    normed = round_value(rms_norm(x, g_mix))
    projected = tapped(product(normed, w_in), probes[0])
    gate_z = projected[:, :DI]
    conv_in = projected[:, DI : 2 * DI + 2 * NS]
    step_raw = projected[:, 2 * DI + 2 * NS :]
    conv = conv_b[None, :] + conv_w[0][None, :] * conv_in
    for lag in range(1, CONV):
        moved = jnp.concatenate(
            [jnp.zeros((lag, conv_in.shape[1]), conv_in.dtype), conv_in[: count - lag]], 0
        )
        keep_rows = (position >= lag).astype(conv_in.dtype)
        conv = conv + conv_w[lag][None, :] * moved * keep_rows[:, None]
    conv = jax.nn.silu(conv)
    ssm_in = conv[:, :DI].reshape(count, NH, MH).transpose(1, 0, 2)
    b_proj = conv[:, DI : DI + NS]
    c_proj = conv[:, DI + NS :]
    step_size = jax.nn.softplus(step_raw + dt_bias[None, :]).T
    decay_sum = lax.dot_general(
        step_size * (-jnp.exp(a_log))[:, None],
        earlier.astype(jnp.float32),
        (((1,), (1,)), ((), ())),
        precision=lax.Precision.HIGHEST,
    )
    cb_scores = contract("tn,sn->ts", c_proj, b_proj)
    inside = visible[None]
    log_gap = jnp.where(inside, decay_sum[:, :, None] - decay_sum[:, None, :], -1e30)
    mix_weight = jnp.exp(log_gap) * cb_scores[None]
    ssm_out = contract("hts,hsp->htp", mix_weight, ssm_in * step_size[:, :, None])
    ssm_out = ssm_out + d_skip[:, None, None] * ssm_in
    ssm_out = ssm_out.transpose(1, 0, 2).reshape(count, DI) * jax.nn.silu(gate_z)
    gated = round_value(rms_norm(ssm_out, g_ssm))
    mixer = product(gated, w_out)
    qkv = tapped(product(normed, w_qkv), probes[1])
    angle_pos = position.astype(jnp.float32)
    query = rotate(qkv[:, : QH * AH].reshape(count, QH, AH), angle_pos).reshape(
        count, KVH, QH // KVH, AH
    )
    key = rotate(qkv[:, QH * AH : (QH + KVH) * AH].reshape(count, KVH, AH), angle_pos)
    value = qkv[:, (QH + KVH) * AH :].reshape(count, KVH, AH)
    query = round_value(query)
    key = round_value(key)
    value = round_value(value)
    scores = contract("tgqa,sga->gqts", query, key) * AH ** (-0.5)
    scores = jnp.where(visible[None, None], scores, -1e30)
    probs = round_value(jax.nn.softmax(scores, axis=-1))
    context = contract("gqts,sga->tgqa", probs, value).reshape(count, QH * AH)
    context = round_value(context)
    middle = x + tapped(mixer + product(context, w_o), probes[2])
    ffn_in = round_value(rms_norm(middle, g_ffn))
    both = tapped(product(ffn_in, w_gu), probes[3])
    action = round_value(jax.nn.silu(both[:, :FF]) * both[:, FF:])
    result = round_value(middle + product(action, w_down))
    lefts = tuple(v.astype(jnp.bfloat16) for v in (normed, gated, context, ffn_in, action))
    return result, lefts


def partial_layer(docs_here, large):

    def apply_layer(layer_in, small, probes):
        return layer(layer_in, small, probes, docs_here, large)

    return apply_layer


def local(
    tokens,
    cotangent,
    lengths,
    w_in,
    conv_w,
    conv_b,
    dt_bias,
    a_log,
    d_skip,
    g_mix,
    g_ssm,
    w_out,
    w_qkv,
    w_o,
    g_ffn,
    w_gu,
    w_down,
):
    first = lax.axis_index("section") == 0
    large = tuple((w[0] for w in (w_in, w_out, w_qkv, w_o, w_gu, w_down)))
    small = tuple(
        (w[0] for w in (conv_w, conv_b, dt_bias, a_log, d_skip, g_mix, g_ssm, g_ffn))
    )
    widths = (large[0].shape[1], large[2].shape[1], D, 2 * FF)
    probes = tuple((jnp.zeros((MB_TOK, width), jnp.float32) for width in widths))
    inputs = tokens.astype(jnp.float32).reshape(MICRO, MB_TOK, D)
    incoming = cotangent.astype(jnp.float32).reshape(MICRO, MB_TOK, D)
    doc_table = jnp.stack([segments(lengths[0, index]) for index in range(MICRO)])
    received = jnp.zeros((MB_TOK, D), jnp.float32)
    results = []
    backers = []
    lefts = []
    for tick in range(MICRO + 1):
        fresh = inputs[min(tick, MICRO - 1)]
        layer_in = jnp.where(first, fresh, received)
        docs_here = jnp.where(first, doc_table[min(tick, MICRO - 1)], doc_table[max(tick - 1, 0)])
        result, backer, left = jax.vjp(
            partial_layer(docs_here, large), layer_in, small, probes, has_aux=True
        )
        lefts.append(left)
        results.append(result)
        backers.append(backer)
        if tick < MICRO:
            received = passed_along(result.astype(jnp.bfloat16), "section", 1).astype(jnp.float32)
    returned = jnp.zeros((MB_TOK, D), jnp.float32)
    input_grads = [None] * (MICRO + 1)
    local_small = [jnp.zeros_like(w) for w in small]
    rights = [None] * (MICRO + 1)
    for tick in reversed(range(MICRO + 1)):
        if tick >= 1:
            seed_grad = incoming[tick - 1]
        else:
            seed_grad = jnp.zeros((MB_TOK, D), jnp.float32)
        upstream = jnp.where(first, returned, seed_grad)
        grad_raw, grads, taps = backers[tick](upstream)
        rights[tick] = tuple(
            (
                v.astype(jnp.bfloat16)
                for v in (jnp.concatenate([taps[0], taps[1]], 1), taps[2], taps[3], upstream)
            )
        )
        grad_in = round_plain(grad_raw)
        input_grads[tick] = grad_in
        if tick > 0:
            returned = passed_along(grad_in.astype(jnp.bfloat16), "section", -1).astype(jnp.float32)
        local_small = [total + grad for total, grad in zip(local_small, grads)]

    def both_blocks(blocks, which):
        return jnp.concatenate(
            [jnp.where(first, blocks[i][which], blocks[i + 1][which]) for i in range(MICRO)], 0
        )

    def weight_grad(which_left, which_right):
        left = both_blocks(lefts, which_left)
        right = both_blocks(rights, which_right)
        columns = right.shape[1]
        right = jnp.pad(right, ((0, 0), (0, -columns % 128)))
        local_sum = lax.dot_general(
            left, right, (((0,), (0,)), ((), ())), preferred_element_type=jnp.float32
        ).astype(jnp.bfloat16)
        summed = lax.psum_scatter(local_sum, "dp", scatter_dimension=0, tiled=True)
        return summed[:, :columns].astype(jnp.float32)[None]

    grad_w_down = weight_grad(4, 3)
    grad_w_gu = weight_grad(3, 2)
    grad_w_out = weight_grad(1, 1)
    grad_w_o = weight_grad(2, 1)
    grad_w_in_qkv = weight_grad(0, 0)
    grad_w_in = grad_w_in_qkv[:, :, : widths[0]]
    grad_w_qkv = grad_w_in_qkv[:, :, widths[0] :]
    packed = jnp.concatenate([grad.reshape(-1) for grad in local_small])
    packed = lax.psum(packed, "dp")
    summed_small = []
    start = 0
    for weight in small:
        summed_small.append(packed[start : start + weight.size].reshape((1,) + weight.shape))
        start += weight.size

    def own_part(whole):
        part = whole.shape[1] // lax.axis_size("dp")
        return lax.dynamic_slice_in_dim(whole, lax.axis_index("dp") * part, part, 1)

    out_rows = [jnp.where(first, results[index], results[index + 1]) for index in range(MICRO)]
    grad_rows = [
        jnp.where(first, input_grads[index], input_grads[index + 1]) for index in range(MICRO)
    ]
    layer_out = jnp.concatenate(out_rows, 0)[None].astype(jnp.bfloat16)
    input_grad = jnp.concatenate(grad_rows, 0)[None].astype(jnp.bfloat16)
    grad_conv_w, grad_conv_b, grad_dt_bias, grad_a_log, grad_d_skip = summed_small[:5]
    grad_g_mix, grad_g_ssm, grad_g_ffn = (own_part(whole) for whole in summed_small[5:])
    return (
        layer_out,
        input_grad,
        grad_w_in,
        grad_conv_w,
        grad_conv_b,
        grad_dt_bias,
        grad_a_log,
        grad_d_skip,
        grad_g_mix,
        grad_g_ssm,
        grad_w_out,
        grad_w_qkv,
        grad_w_o,
        grad_g_ffn,
        grad_w_gu,
        grad_w_down,
    )


def solution(mesh):
    in_specs = (
        P("dp", None),
        P("dp", None),
        P("dp", None, None),
        P("section", None, None),
        P("section", None, None),
        P("section", None),
        P("section", None),
        P("section", None),
        P("section", None),
        P("section", None),
        P("section", None),
        P("section", None, None),
        P("section", None, None),
        P("section", None, None),
        P("section", None),
        P("section", None, None),
        P("section", None, None),
    )
    out_specs = (
        P("section", "dp", None),
        P("section", "dp", None),
        P("section", "dp", None),
        P("section", None, None),
        P("section", None),
        P("section", None),
        P("section", None),
        P("section", None),
        P("section", "dp"),
        P("section", "dp"),
        P("section", "dp", None),
        P("section", "dp", None),
        P("section", "dp", None),
        P("section", "dp"),
        P("section", "dp", None),
        P("section", "dp", None),
    )
    return jax.shard_map(local, mesh=mesh, in_specs=in_specs, out_specs=out_specs, check_vma=False)
```

time: 2100 us -> 969 us (0.46)
  waiting for transfers between devices: 1250 us -> 496 us
  matrix products: 507 us -> 164 us
  local copies, waits for them, and re-layouts: 97.9 us -> 70.1 us
    reduce_scatter x5, waiting for transfers between devices: 904 us -> 493 us  [weight_grad(): summed = lax.psum_scatter(local_sum, 'dp', scatter_dimension=0, tiled=True)]
    unnamed x13 -> x5, waiting for transfers between devices: 349 us -> 0.08 us
    dot_general x90 -> x83, matrix products: 507 us -> 164 us  [the longest x36 44.6 us: contract(): return jnp.einsum(spec, left, right, precision=lax.Precision.DEFAULT)]
    broadcast_in_dim x1 -> x0, local copies, waits for them, and re-layouts: 32.2 us -> none  [local(): g[None]]
    select_n x0 -> x15, other arithmetic: none -> 29.7 us  [the longest x12 28 us: both_blocks(): jnp.where(first, blocks[i][which], blocks[i + 1][which])]
  transfers between devices with their start and end apart: 13 -> 9, of which waited for: 6 -> 6; matrix products, arithmetic and copies ran while one was open for 14% -> 11% of each run, Pallas kernels for 0% -> 0%
where the time goes in v1:
time: 969 us; the launch traced here: 961 us
  waiting for transfers between devices  496 us (51%)
  matrix products  164 us (17%)
  other arithmetic  137 us (14%)
  local copies, waits for them, and re-layouts  70.1 us (7%)
  blocking collectives  65.7 us (7%)
  between operations  18.9 us (2%)
    reduce_scatter x5, waiting for transfers between devices, weight_grad(): summed = lax.psum_scatter(local_sum, 'dp', scatter_dimension=0, tiled=True)  493 us
    psum x1, blocking collectives, local(): packed = lax.psum(packed, 'dp')  65.7 us
    dot_general x36, matrix products, contract(): return jnp.einsum(spec, left, right, precision=lax.Precision.DEFAULT)  44.6 us
    dot_general x18, matrix products, product(): jnp.dot(left.astype(jnp.bfloat16), weight, preferred_element_type=jnp.flo...  37.5 us
    unnamed x746, local copies, waits for them, and re-layouts  35.6 us
    select_n x12, other arithmetic, both_blocks(): jnp.where(first, blocks[i][which], blocks[i + 1][which])  28 us
    dot_general x5, matrix products, weight_grad(): lax.dot_general(left, right, (((0,), (0,)), ((), ())), preferred_element_...  24.2 us
  transfers between devices with their start and end apart: 9, of which 6 were waited for; matrix products, arithmetic and copies ran while one was open for 11% of the time, Pallas kernels for 0%

profile of v1, /device:TPU:10, one launch (start us, length us, event | category | flops | bytes accessed | tf_op | source)
XLA Modules:
  0.0 961.2 jit_solution(17873419457031905790)
XLA Ops:
  12.7 3.2 fusion.169
  16.8 2.5 fusion.24
  25.4 6.5 fusion.146
  48.4 2.6 multiply_reduce_fusion.32
  54.8 2.4 fusion.12
  59.5 3.0 collective-permute-start
  70.0 5.1 fusion.22
  78.8 3.9 fusion.145
  96.5 2.6 multiply_reduce_fusion.31
  106.5 2.4 fusion.10
  115.5 2.4 collective-permute-start.1
  119.6 3.0 convert_element_type.501
  136.0 5.1 fusion.20
  144.0 3.9 fusion.144
  150.9 3.9 bitcast_add_fusion
  160.6 2.4 fusion.8
  163.5 4.0 fusion.288
  167.5 6.3 multiply_reduce_fusion.35
  179.1 4.1 fusion.63
  195.7 2.5 multiply_reduce_fusion.16
  215.4 2.8 broadcast_select_fusion.6
  218.2 5.4 fusion.287
  223.7 8.2 multiply_reduce_fusion.34
  231.9 2.4 broadcast_select_fusion.10
  239.6 4.5 fusion.65
  255.8 2.4 multiply_reduce_fusion.12
  262.4 2.6 fusion.380
  265.2 2.4 fusion.16
  270.5 2.4 fusion.264
  274.5 2.8 collective-permute-done.3
  279.6 3.2 multiply_reduce_fusion.33
  282.9 3.0 broadcast_select_fusion.11
  290.9 3.5 convolution_convert_fusion.3
  294.6 4.5 broadcast_select_fusion.2
  299.1 4.4 convolution_convert_fusion.2
  303.6 5.2 broadcast_select_fusion.1
  308.8 6.8 convolution_convert_fusion.1
  331.4 4.6 fusion.67
  341.8 2.5 multiply_reduce_fusion.8
  352.8 7.8 convolution_convert_fusion
  363.1 4.2 fusion.227
  370.9 5.7 fusion.14
  378.7 65.7 %psum.7 = f32[12616]{0:T(1024)S(1)} all-reduce(f32[12616]{0:T(1024)S(1)} %concatenate.150), channel_id=1, replica_groups=mesh['section'=2,'dp'=16] {'dp'}, use_global_device_ids=true, to_apply=%region_80.82 | all-reduce | flops 12616 | bytes 100928 | tf_op jit(solution)/shard_map/psum | solution.py:257
  447.5 2.5 fusion.265
  453.2 47.7 %reduce-scatter.8.cloned.1.call-done = bf16[96,1024]{1,0:T(8,128)(2,1)} async-done(((bf16[1536,1024]{1,0:T(8,128)(2,1)}), bf16[96,1024]{1,0:T(8,128)(2,1)}) %reduce-scatter.8.cloned.1.call-update) | async-done | bytes 196624 | tf_op jit(solution)/shard_map/reduce_scatter | solution.py:246
  502.6 94.7 %reduce-scatter.14.cloned.1.call-done = bf16[128,1024]{1,0:T(8,128)(2,1)} async-done(((bf16[2048,1024]{1,0:T(8,128)(2,1)}), bf16[128,1024]{1,0:T(8,128)(2,1)}) %reduce-scatter.14.cloned.1.call-update) | async-done | bytes 262160 | tf_op jit(solution)/shard_map/reduce_scatter | solution.py:246
  599.1 181.4 %reduce-scatter.12.cloned.1.call-done = bf16[64,4096]{1,0:T(8,128)(2,1)} async-done(((bf16[1024,4096]{1,0:T(8,128)(2,1)}), bf16[64,4096]{1,0:T(8,128)(2,1)}) %reduce-scatter.12.cloned.1.call-update) | async-done | bytes 524304 | tf_op jit(solution)/shard_map/reduce_scatter | solution.py:246
  782.6 168.9 %reduce-scatter.6.cloned.1.call-done = bf16[64,4224]{1,0:T(8,128)(2,1)} async-done(((bf16[1024,4224]{1,0:T(8,128)(2,1)}), bf16[64,4224]{1,0:T(8,128)(2,1)}) %reduce-scatter.6.cloned.1.call-update) | async-done | bytes 540688 | tf_op jit(solution)/shard_map/reduce_scatter | solution.py:246
  (1032 shorter events, 218.7 us)
Async XLA Ops:
  7.2 44.2 %copy-start = (bf16[1,1536,1024]{2,1,0:T(8,128)(2,1)S(1)}, bf16[1,1536,1024]{2,1,0:T(8,128)(2,1)}, u32[]{:S(2)}) copy-start(bf16[1,1536,1024]{2,1,0:T(8,128)(2,1)} %param.29) | copy-start | bytes 9437188
  7.2 444.5 %reduce-scatter.10.cloned.1.call-start = ((), (), s32[]{:S(2)}) async-start(), calls=%async_computation.7 | async-start | bytes 1114112 | tf_op jit(solution)/shard_map/reduce_scatter | solution.py:246
  9.9 15.4 %copy-start.291 = (f32[256]{0:T(256)}, f32[256]{0:T(256)S(1)}, u32[]{:S(2)}) copy-start(f32[256]{0:T(256)S(1)} %get-tuple-element.213) | copy-start | bytes 3076
  9.9 15.4 %copy-start.293 = (f32[256]{0:T(256)}, f32[256]{0:T(256)S(1)}, u32[]{:S(2)}) copy-start(f32[256]{0:T(256)S(1)} %get-tuple-element.214) | copy-start | bytes 3076
  9.9 15.4 %copy-start.295 = (f32[256]{0:T(256)}, f32[256]{0:T(256)S(1)}, u32[]{:S(2)}) copy-start(f32[256]{0:T(256)S(1)} %get-tuple-element.215) | copy-start | bytes 3076
  10.7 34.1 %copy-start.108 = (pred[256,256]{0,1:T(8,128)(4,1)}, pred[256,256]{0,1:T(8,128)(4,1)S(1)}, u32[]{:S(2)}) copy-start(pred[256,256]{0,1:T(8,128)(4,1)S(1)} %get-tuple-element.200) | copy-start | bytes 196612
  10.8 24.2 %copy-start.321 = (s32[256]{0:T(256)}, s32[256]{0:T(256)S(1)}, u32[]{:S(2)}) copy-start(s32[256]{0:T(256)S(1)} %convert_reduce_fusion) | copy-start | bytes 3076
  10.8 24.0 %copy-start.265 = (s32[256]{0:T(256)}, s32[256]{0:T(256)S(1)}, u32[]{:S(2)}) copy-start(s32[256]{0:T(256)S(1)} %broadcast_select_fusion.16) | copy-start | bytes 3076
  37.0 14.0 %copy-start.140 = (bf16[256,128]{0,1:T(8,128)(2,1)}, bf16[256,128]{0,1:T(8,128)(2,1)S(1)}, u32[]{:S(2)}) copy-start(bf16[256,128]{0,1:T(8,128)(2,1)S(1)} %copy.97) | copy-start | bytes 196612
  41.0 49.3 %copy-start.135 = (f32[256,32]{0,1:T(8,128)}, f32[256,32]{0,1:T(8,128)S(1)}, u32[]{:S(2)}) copy-start(f32[256,32]{0,1:T(8,128)S(1)} %get-tuple-element.216) | copy-start | bytes 98308
  41.0 49.3 %copy-start.137 = (f32[256,32]{0,1:T(8,128)}, f32[256,32]{0,1:T(8,128)S(1)}, u32[]{:S(2)}) copy-start(f32[256,32]{0,1:T(8,128)S(1)} %get-tuple-element.217) | copy-start | bytes 98308
  59.5 4.6 collective-permute-start
  63.3 29.7 %copy-start.110 = (pred[256,256]{0,1:T(8,128)(4,1)}, pred[256,256]{0,1:T(8,128)(4,1)S(1)}, u32[]{:S(2)}) copy-start(pred[256,256]{0,1:T(8,128)(4,1)S(1)} %get-tuple-element.202) | copy-start | bytes 196612
  64.0 13.4 %copy-start.297 = (f32[256]{0:T(256)}, f32[256]{0:T(256)S(1)}, u32[]{:S(2)}) copy-start(f32[256]{0:T(256)S(1)} %get-tuple-element.208) | copy-start | bytes 3076
  64.0 13.4 %copy-start.299 = (f32[256]{0:T(256)}, f32[256]{0:T(256)S(1)}, u32[]{:S(2)}) copy-start(f32[256]{0:T(256)S(1)} %get-tuple-element.209) | copy-start | bytes 3076
  64.1 13.4 %copy-start.301 = (f32[256]{0:T(256)}, f32[256]{0:T(256)S(1)}, u32[]{:S(2)}) copy-start(f32[256]{0:T(256)S(1)} %get-tuple-element.210) | copy-start | bytes 3076
  86.3 15.3 %copy-start.142 = (bf16[256,128]{0,1:T(8,128)(2,1)}, bf16[256,128]{0,1:T(8,128)(2,1)S(1)}, u32[]{:S(2)}) copy-start(bf16[256,128]{0,1:T(8,128)(2,1)S(1)} %copy.102) | copy-start | bytes 196612
  93.7 7.9 copy-start.75
  99.1 7.4 slice-start.6
  103.7 7.9 copy-start.78
  115.5 7.1 copy-start.322
  115.5 7.7 collective-permute-start.1
  133.6 7.5 copy-start.214
  141.2 9.5 copy-start.278
  150.9 28.1 %copy-start.359 = (f32[24,256]{1,0:T(8,128)}, f32[24,256]{1,0:T(8,128)S(1)}, u32[]{:S(2)}) copy-start(f32[24,256]{1,0:T(8,128)S(1)} %fusion.280) | copy-start | bytes 73732
  156.0 21.6 %copy-start.19 = (f32[256,1536]{0,1:T(8,128)}, f32[256,1536]{0,1:T(8,128)S(1)}, u32[]{:S(2)}) copy-start(f32[256,1536]{0,1:T(8,128)S(1)} %get-tuple-element.120) | copy-start | bytes 4718596
  156.0 21.6 %copy-start.255 = (f32[256]{0:T(256)}, f32[256]{0:T(256)S(1)}, u32[]{:S(2)}) copy-start(f32[256]{0:T(256)S(1)} %fusion.345) | copy-start | bytes 3076
  159.7 14.1 %copy-start.46 = (f32[256,1024]{1,0:T(8,128)}, f32[256,1024]{1,0:T(8,128)S(1)}, u32[]{:S(2)}) copy-start(f32[256,1024]{1,0:T(8,128)S(1)} %get-tuple-element.231) | copy-start | bytes 3145732
  159.7 14.1 %copy-start.263 = (f32[256]{0:T(256)}, f32[256]{0:T(256)S(1)}, u32[]{:S(2)}) copy-start(f32[256]{0:T(256)S(1)} %fusion.346) | copy-start | bytes 3076
  175.6 34.6 %copy-start.37 = (f32[256,1024]{1,0:T(8,128)}, f32[256,1024]{1,0:T(8,128)S(1)}, u32[]{:S(2)}) copy-start(f32[256,1024]{1,0:T(8,128)S(1)} %add_add_fusion.8) | copy-start | bytes 3145732
  211.3 4.1 collective-permute-start.2
  223.6 8.3 copy-start.122
  223.6 8.2 copy-start.123
  223.7 8.2 copy-start.318
  223.7 8.2 copy-start.38
  223.7 8.2 copy-start.72
  239.6 7.3 copy-start.207
  269.1 8.2 copy-start.343
  272.9 4.3 collective-permute-start.3
  288.5 212.4 %reduce-scatter.8.cloned.1.call-start = ((), (), s32[]{:S(2)}) async-start(), calls=%async_computation.6 | async-start | bytes 3342336 | tf_op jit(solution)/shard_map/reduce_scatter | solution.py:246
  294.4 302.9 %reduce-scatter.14.cloned.1.call-start = ((), (), s32[]{:S(2)}) async-start(), calls=%async_computation.9 | async-start | bytes 4456448 | tf_op jit(solution)/shard_map/reduce_scatter | solution.py:246
  303.5 477.0 %reduce-scatter.12.cloned.1.call-start = ((), (), s32[]{:S(2)}) async-start(), calls=%async_computation.8 | async-start | bytes 8912896 | tf_op jit(solution)/shard_map/reduce_scatter | solution.py:246
  315.6 635.9 %reduce-scatter.6.cloned.1.call-start = ((), (), s32[]{:S(2)}) async-start(), calls=%async_computation.5 | async-start | bytes 9191424 | tf_op jit(solution)/shard_map/reduce_scatter | solution.py:246
  324.9 24.2 %copy-start.105 = (bf16[256,768]{0,1:T(8,128)(2,1)}, bf16[256,768]{0,1:T(8,128)(2,1)S(1)}, u32[]{:S(2)}) copy-start(bf16[256,768]{0,1:T(8,128)(2,1)S(1)} %add_convert_fusion.6) | copy-start | bytes 1179652
  331.4 8.3 copy-start.66
  331.4 8.3 copy-start.85
  331.4 8.3 copy-start.296
  376.8 70.7 %copy-start.310 = (f32[256]{0:T(256)S(1)}, f32[256]{0:T(256)}, u32[]{:S(2)}) copy-start(f32[256]{0:T(256)} %copy-done.309) | copy-start | bytes 3076
  (334 other events, 808.1 us)
Sparse Core Ops, SparseCore 0:
  288.6 68.1 reduce-scatter.9
  362.5 138.3 reduce-scatter.7
  503.3 93.9 reduce-scatter.13
  599.6 180.9 reduce-scatter.11
  787.0 164.4 reduce-scatter.5
